TPU v7x, 32 devices: a whole 2x2x4 slice. The times are simulated.
32 devices in a mesh: cells: 8 (over z, y), tiles: 4 (over x, core).
Axes of the slice: x: 2, y: 2, z: 4, core: 2. Of those that a mesh axis runs over, the one named last changes fastest.
Arguments:
- embeddings: bfloat16 [3, 8192, 256], P(None, 'cells'), may hold values from -6 to 6
- log_mass: float32 [3, 8192], P(None, 'cells'), may hold values from -1 to 1
- signatures: bfloat16 [8192, 256], P('cells'), may hold values from -6 to 6
- tile_list: int32 [2, 2, 1024], P(None, None, ('cells', 'tiles')), may hold values from -1 to 63, as said below
Outputs:
- early_fates: bfloat16 [8192, 256], P('cells')
- late_fates: bfloat16 [8192, 256], P('cells')
Inputs may be any that keep to these rules, and one draw needn't show every extreme that they name: `tile_list`: for each coupling, slots c * 128 to c * 128 + 127 belong to owner c (an index of cells). A live slot holds a source block of owner c (blocks c * 8 to c * 8 + 7) and a target block of owner c - 1, c or c + 1; an empty slot holds -1 in both rows. Within the slots of each device the live ones come first. No pair of blocks appears twice in a coupling, every source block and every target block appears in some live slot, and one owner in each coupling has all 128 slots live.
All inputs are finite; a program needn't handle non-finite values.
Results may differ from a plain program's by a relative error of at most 0.006.
Values may be sent and summed in bfloat16 or wider, within the bound.
A program may use at most 64 MiB of HBM per device.

v0:
```python
import functools
import math

import jax
import jax.numpy as jnp
from jax import lax
from jax.experimental import pallas as pl
from jax.experimental.pallas import tpu as pltpu
from jax.sharding import PartitionSpec as P

BLOCK = 128
SWEEPS = 2
EPS = 0.01
RHO = 1.0
NEG = -1e30
LOG2E = math.log2(math.e)
LAM = RHO / (RHO + EPS)
F32 = jnp.float32
BF16 = jnp.bfloat16
NT = (((1,), (1,)), ((), ()))


def copy_count(tiles):
    return tiles * 12 + 40


def kernel(
    tiles,
    emb,
    log_mass,
    sig,
    listing,
    early,
    late,
    xs,
    ys,
    d,
    dt,
    fates_1,
    fates_0,
    w_0,
    lists,
    lm_src,
    lm_win,
    bias,
    x_norm,
    y_norm,
    h_row,
    hb,
    ub,
    row_send,
    row_recv,
    col_send,
    col_near,
    col_far,
    part_send,
    part_recv,
    own_part,
    early_own,
    send_sem,
    recv_sem,
    local_sem,
):
    c = lax.axis_index("cells")
    t = lax.axis_index("tiles")
    n = lax.axis_size("cells")
    rows = xs.shape[1]
    depth = xs.shape[2]
    q_rows = ys.shape[2]
    n_src = rows // BLOCK
    n_q = q_rows // BLOCK
    n_tgt = 3 * n_q
    scale = LOG2E / (EPS * depth)
    t_rows = pl.ds(pl.multiple_of(t * q_rows, q_rows), q_rows)

    counter = [0]
    sends = []

    def fresh():
        counter[0] += 1
        return counter[0] - 1

    def present(offset):
        return jnp.logical_and(c + offset >= 0, c + offset < n)

    def to_tile(src, dst, step):
        i = fresh()
        copy = pltpu.make_async_remote_copy(
            src_ref=src,
            dst_ref=dst,
            send_sem=send_sem.at[i],
            recv_sem=recv_sem.at[i],
            device_id={"tiles": lax.rem(t + step, tiles)},
            device_id_type=pl.DeviceIdType.MESH,
        )
        copy.start()
        sends.append((copy, None))
        return copy.wait_recv

    def to_cell(src, dst, offset):
        i = fresh()
        copy = pltpu.make_async_remote_copy(
            src_ref=src,
            dst_ref=dst,
            send_sem=send_sem.at[i],
            recv_sem=recv_sem.at[i],
            device_id={"cells": c + offset},
            device_id_type=pl.DeviceIdType.MESH,
        )

        @pl.when(present(offset))
        def _():
            copy.start()

        sends.append((copy, offset))

        def wait():
            @pl.when(present(-offset))
            def _():
                copy.wait_recv()

        return wait

    for offset, part in ((1, 0), (-1, 2)):

        @pl.when(jnp.logical_not(present(-offset)))
        def _(part=part):
            for k in range(2):
                ys[k, part] = jnp.zeros(ys.shape[2:], BF16)
            fates_1[part] = jnp.zeros(fates_1.shape[1:], BF16)
            fates_0[part] = jnp.zeros(fates_0.shape[1:], BF16)
            lm_win[part] = jnp.zeros(lm_win.shape[1:], F32)

    for buffer in (col_near, col_far):
        buffer[:, :, :, :, 0] = jnp.full(buffer.shape[:4] + buffer.shape[5:], NEG, F32)
        buffer[:, :, :, :, 1] = jnp.zeros(buffer.shape[:4] + buffer.shape[5:], F32)
    col_send[:, :, :, 0] = jnp.full(col_send.shape[:3] + col_send.shape[4:], NEG, F32)
    col_send[:, :, :, 1] = jnp.ones(col_send.shape[:3] + col_send.shape[4:], F32)

    barrier = pltpu.get_barrier_semaphore()
    for step in range(1, tiles):
        pl.semaphore_signal(
            barrier, inc=1, device_id={"tiles": lax.rem(t + step, tiles)}, device_id_type=pl.DeviceIdType.MESH
        )
    for offset in (1, -1, 2, -2):

        @pl.when(present(offset))
        def _(offset=offset):
            pl.semaphore_signal(
                barrier, inc=1, device_id={"cells": c + offset}, device_id_type=pl.DeviceIdType.MESH
            )

    local = []
    for i, (src, dst) in enumerate(
        (
            (emb.at[1], xs.at[1]),
            (emb.at[2, t_rows], ys.at[1, 1]),
            (emb.at[0], xs.at[0]),
            (emb.at[1, t_rows], ys.at[0, 1]),
            (sig.at[t_rows], fates_1.at[1]),
        )
    ):
        copy = pltpu.make_async_copy(src, dst, local_sem.at[i])
        copy.start()
        local.append(copy)

    lm_src[...] = jnp.zeros(lm_src.shape, F32)
    for k in range(2):
        for q in range(n_q):
            lanes = pl.ds(pl.multiple_of((t * n_q + q) * BLOCK, BLOCK), BLOCK)
            lm_src[k, q : q + 1, :] = log_mass[k + 1 : k + 2, lanes] * LOG2E
    lm_win[1] = lm_src[...]

    peers = sum(present(offset).astype(jnp.int32) for offset in (1, -1, 2, -2))
    pl.semaphore_wait(barrier, tiles - 1 + peers)

    list_waits = [to_tile(listing, lists.at[step], step) for step in range(1, tiles)]
    near = ((1, 0), (-1, 2))
    lm_waits = [to_cell(lm_src, lm_win.at[part], offset) for offset, part in near]
    y_waits = [None, None]
    y_waits[1] = [to_cell(emb.at[2, t_rows], ys.at[1, part], offset) for offset, part in near]
    y_waits[0] = [to_cell(emb.at[1, t_rows], ys.at[0, part], offset) for offset, part in near]
    sig_waits = [to_cell(sig.at[t_rows], fates_1.at[part], offset) for offset, part in near]

    lists[0] = listing[...]
    for wait in list_waits:
        wait()

    pair = lax.broadcasted_iota(jnp.int32, (n_src * n_tgt, 1), 0)
    src_id = c * n_src + pair // n_tgt
    slot = pair % n_tgt
    tgt_id = (c - 1 + slot // n_q) * n_src + t * n_q + slot % n_q
    for k in range(2):
        found = jnp.zeros((n_src * n_tgt, 1), F32)
        for step in range(tiles):
            hit = jnp.logical_and(
                lists[step, k, 0:1, :] == src_id, lists[step, k, 1:2, :] == tgt_id
            )
            found = found + jnp.sum(jnp.where(hit, 1.0, 0.0), axis=1, keepdims=True)
        bias[k] = jnp.broadcast_to(jnp.where(found > 0.0, 0.0, NEG), (n_src * n_tgt, BLOCK))

    ones = jnp.ones((8, depth), BF16)

    def norm_rows(block):
        wide = block.astype(F32)
        square = wide * wide
        high = square.astype(BF16)
        low = (square - high.astype(F32)).astype(BF16)
        return scale * (
            lax.dot_general(ones, high, NT, preferred_element_type=F32)
            + lax.dot_general(ones, low, NT, preferred_element_type=F32)
        )

    def source_norms(k):
        @pl.loop(0, n_src)
        def _(b):
            x_norm[k, pl.ds(b, 1), :] = norm_rows(xs[k, pl.ds(pl.multiple_of(b * BLOCK, BLOCK), BLOCK), :])[0:1]

    def products(k, part):
        y = ys[k, part]
        norms = norm_rows(y)
        for q in range(n_q):
            y_norm[k, part, q : q + 1, :] = norms[0:1, q * BLOCK : (q + 1) * BLOCK]

        @pl.loop(0, n_src)
        def _(b):
            block = pl.ds(pl.multiple_of(b * BLOCK, BLOCK), BLOCK)
            x = xs[k, block, :]
            cross = lax.dot_general(x, y, NT, preferred_element_type=F32) * (2.0 * scale)
            crossed = lax.dot_general(y, x, NT, preferred_element_type=F32) * (2.0 * scale)
            for q in range(n_q):
                j = part * n_q + q
                shift = bias[k, pl.ds(b * n_tgt + j, 1), :]
                d[k, j, block, :] = cross[:, q * BLOCK : (q + 1) * BLOCK] + shift
                dt[k, b, j * BLOCK : (j + 1) * BLOCK, :] = crossed[q * BLOCK : (q + 1) * BLOCK] + shift

    def down(row):
        return jnp.transpose(jnp.broadcast_to(row, (BLOCK, BLOCK)))

    def row_pass(k, phase):
        for j in range(n_tgt):
            hb[k, j * BLOCK : (j + 1) * BLOCK, :] = down(h_row[k, j // n_q, j % n_q : j % n_q + 1, :])

        @pl.loop(0, n_src)
        def _(b):
            scores = hb[k] + dt[k, b]
            highest = jnp.max(scores, axis=0, keepdims=True)
            row_send[k, phase, 0, pl.ds(b, 1), :] = highest
            row_send[k, phase, 1, pl.ds(b, 1), :] = jnp.sum(jnp.exp2(scores - highest), axis=0, keepdims=True)

        return [
            to_tile(row_send.at[k, phase], row_recv.at[k, phase, step - 1], step) for step in range(1, tiles)
        ]

    def merged(pairs):
        highest = functools.reduce(jnp.maximum, [pair[0] for pair in pairs])
        total = sum(pair[1] * jnp.exp2(pair[0] - highest) for pair in pairs)
        return highest + jnp.log(total) * LOG2E

    def row_total(k, phase, waits):
        for wait in waits:
            wait()
        pairs = [(row_send[k, phase, 0], row_send[k, phase, 1])]
        pairs += [(row_recv[k, phase, s, 0], row_recv[k, phase, s, 1]) for s in range(tiles - 1)]
        return merged(pairs)

    def spread(k, values):
        for b in range(n_src):
            ub[k, b * BLOCK : (b + 1) * BLOCK, :] = down(values[b : b + 1])

    def col_pass(k, phase, total):
        mass = jnp.concatenate(
            [log_mass[k : k + 1, b * BLOCK : (b + 1) * BLOCK] for b in range(n_src)], axis=0
        )
        spread(k, mass * LOG2E - LAM * total + (LAM - 1.0) * x_norm[k])

        @pl.loop(0, 3)
        def _(part):
            for q in range(n_q):
                scores = ub[k] + d[k, part * n_q + q]
                highest = jnp.max(scores, axis=0, keepdims=True)
                col_send[k, phase, part, 0, q : q + 1, :] = highest
                col_send[k, phase, part, 1, q : q + 1, :] = jnp.sum(
                    jnp.exp2(scores - highest), axis=0, keepdims=True
                )

        mine = col_send.at[k, phase]
        return [
            to_cell(mine.at[pl.ds(1, 2)], col_near.at[k, phase, 0], 1),
            to_cell(mine.at[pl.ds(0, 2)], col_near.at[k, phase, 1], -1),
            to_cell(mine.at[pl.ds(2, 1)], col_far.at[k, phase, 0], 2),
            to_cell(mine.at[pl.ds(0, 1)], col_far.at[k, phase, 1], -2),
        ]

    def col_total(k, phase, waits):
        for wait in waits:
            wait()

        def pair(ref):
            return ref[0], ref[1]

        mine = col_send.at[k, phase]
        below, above = col_near.at[k, phase, 0], col_near.at[k, phase, 1]
        far_below, far_above = col_far.at[k, phase, 0, 0], col_far.at[k, phase, 1, 0]
        totals = (
            merged([pair(far_below), pair(below.at[0]), pair(mine.at[0])]),
            merged([pair(below.at[1]), pair(mine.at[1]), pair(above.at[0])]),
            merged([pair(mine.at[2]), pair(above.at[1]), pair(far_above)]),
        )
        for part in range(3):
            h_row[k, part] = lm_win[part, k] - LAM * totals[part] + (LAM - 1.0) * y_norm[k, part]

    y_norm[...] = jnp.zeros(y_norm.shape, F32)
    local[0].wait()
    local[1].wait()
    source_norms(1)
    products(1, 1)
    local[2].wait()
    local[3].wait()
    source_norms(0)
    products(0, 1)
    for wait in lm_waits:
        wait()
    row_waits, col_waits = {}, {}
    for k in (1, 0):
        for wait, (_, part) in zip(y_waits[k], near):
            wait()
            products(k, part)
        for part in range(3):
            h_row[k, part] = lm_win[part, k] - y_norm[k, part]
        row_waits[k] = row_pass(k, 0)
    for sweep in range(SWEEPS):
        for k in (1, 0):
            col_waits[k] = col_pass(k, sweep, row_total(k, sweep, row_waits[k]))
        for k in (1, 0):
            col_total(k, sweep, col_waits[k])
            row_waits[k] = row_pass(k, sweep + 1)

    def weights(k, block, part):
        return jnp.concatenate(
            [
                jnp.exp2(
                    h_row[k, part, q : q + 1, :] + d[k, part * n_q + q, block, :] - ub[k, block, :]
                ).astype(BF16)
                for q in range(n_q)
            ],
            axis=1,
        )

    def row_block(index):
        return pl.ds(pl.multiple_of(index * q_rows, q_rows), q_rows)

    spread(1, row_total(1, SWEEPS, row_waits[1]))
    local[4].wait()
    for wait in sig_waits:
        wait()
    part_waits = []
    for step in range(1, tiles + 1):
        block = row_block(lax.rem(t + step, tiles))
        total = sum(
            jnp.dot(weights(1, block, part), fates_1[part], preferred_element_type=F32) for part in range(3)
        )
        if step < tiles:
            part_send[1, step - 1] = total.astype(BF16)
            part_waits.append(to_tile(part_send.at[1, step - 1], part_recv.at[1, step - 1], step))
        else:
            own_part[...] = total

    spread(0, row_total(0, SWEEPS, row_waits[0]))

    @pl.loop(0, tiles)
    def _(r):
        block = row_block(r)
        for part in range(3):
            w_0[part, block, :] = weights(0, block, part)

    for wait in part_waits:
        wait()
    fates_0[1] = (
        own_part[...] + sum(part_recv[1, s].astype(F32) for s in range(tiles - 1))
    ).astype(BF16)
    late_waits = [to_cell(fates_0.at[1], fates_0.at[part], offset) for offset, part in near]
    gather_waits = [to_tile(fates_0.at[1], late.at[t_rows], step) for step in range(1, tiles)]
    late[t_rows, :] = fates_0[1]

    for wait in late_waits:
        wait()
    part_waits = []
    for step in range(1, tiles + 1):
        block = row_block(lax.rem(t + step, tiles))
        total = sum(
            jnp.dot(w_0[part, block, :], fates_0[part], preferred_element_type=F32) for part in range(3)
        )
        if step < tiles:
            part_send[0, step - 1] = total.astype(BF16)
            part_waits.append(to_tile(part_send.at[0, step - 1], part_recv.at[0, step - 1], step))
        else:
            own_part[...] = total
    for wait in part_waits:
        wait()
    early_own[...] = (
        own_part[...] + sum(part_recv[0, s].astype(F32) for s in range(tiles - 1))
    ).astype(BF16)
    gather_waits += [to_tile(early_own, early.at[t_rows], step) for step in range(1, tiles)]
    early[t_rows, :] = early_own[...]
    for wait in gather_waits:
        wait()
    for copy, offset in sends:
        if offset is None:
            copy.wait_send()
        else:

            @pl.when(present(offset))
            def _(copy=copy):
                copy.wait_send()


def on_device(tiles, embeddings, log_mass, signatures, tile_list):
    _, rows, depth = embeddings.shape
    fate = signatures.shape[1]
    q_rows = rows // tiles
    n_src = rows // BLOCK
    n_q = q_rows // BLOCK
    n_tgt = 3 * n_q
    vmem = pltpu.VMEM
    copies = copy_count(tiles)
    return pl.pallas_call(
        functools.partial(kernel, tiles),
        out_shape=(
            jax.ShapeDtypeStruct((rows, fate), BF16),
            jax.ShapeDtypeStruct((rows, fate), BF16),
        ),
        in_specs=[
            pl.BlockSpec(memory_space=pl.ANY),
            pl.BlockSpec(memory_space=vmem),
            pl.BlockSpec(memory_space=pl.ANY),
            pl.BlockSpec(memory_space=vmem),
        ],
        out_specs=(pl.BlockSpec(memory_space=vmem), pl.BlockSpec(memory_space=vmem)),
        scratch_shapes=[
            vmem((2, rows, depth), BF16),
            vmem((2, 3, q_rows, depth), BF16),
            vmem((2, n_tgt, rows, BLOCK), F32),
            vmem((2, n_src, n_tgt * BLOCK, BLOCK), F32),
            vmem((3, q_rows, fate), BF16),
            vmem((3, q_rows, fate), BF16),
            vmem((3, rows, q_rows), BF16),
            vmem((tiles,) + tile_list.shape, jnp.int32),
            vmem((2, 8, BLOCK), F32),
            vmem((3, 2, 8, BLOCK), F32),
            vmem((2, n_src * n_tgt, BLOCK), F32),
            vmem((2, n_src, BLOCK), F32),
            vmem((2, 3, 8, BLOCK), F32),
            vmem((2, 3, 8, BLOCK), F32),
            vmem((2, n_tgt * BLOCK, BLOCK), F32),
            vmem((2, rows, BLOCK), F32),
            vmem((2, SWEEPS + 1, 2, n_src, BLOCK), F32),
            vmem((2, SWEEPS + 1, tiles - 1, 2, n_src, BLOCK), F32),
            vmem((2, SWEEPS, 3, 2, 8, BLOCK), F32),
            vmem((2, SWEEPS, 2, 2, 2, 8, BLOCK), F32),
            vmem((2, SWEEPS, 2, 1, 2, 8, BLOCK), F32),
            vmem((2, tiles - 1, q_rows, fate), BF16),
            vmem((2, tiles - 1, q_rows, fate), BF16),
            vmem((q_rows, fate), F32),
            vmem((q_rows, fate), BF16),
            pltpu.SemaphoreType.DMA((copies,)),
            pltpu.SemaphoreType.DMA((copies,)),
            pltpu.SemaphoreType.DMA((5,)),
        ],
        compiler_params=pltpu.CompilerParams(
            collective_id=0, has_side_effects=True, vmem_limit_bytes=44 * 1024 * 1024
        ),
    )(embeddings, log_mass, signatures, tile_list)


def solution(mesh):
    in_specs = (
        P(None, "cells", None),
        P(None, "cells"),
        P("cells", None),
        P(None, None, ("cells", "tiles")),
    )
    out_specs = (P("cells", None), P("cells", None))
    return jax.shard_map(
        functools.partial(on_device, mesh.shape["tiles"]),
        mesh=mesh,
        in_specs=in_specs,
        out_specs=out_specs,
        check_vma=False,
    )
```

profile of v0, /device:TPU:9, one launch (start us, length us, event | category | flops | bytes accessed | tf_op | source)
XLA Modules:
  0.0 82.6 jit_solution(14669171394458401265)
XLA Ops:
  0.6 0.0 copy-start
  0.6 1.4 %copy-done = bf16[3,1024,256]{2,1,0:T(8,128)(2,1)S(1)} copy-done((bf16[3,1024,256]{2,1,0:T(8,128)(2,1)S(1)}, bf16[3,1024,256]{2,1,0:T(8,128)(2,1)}, u32[]{:S(2)}) %copy-start) | copy-done | bytes 1572888
  2.0 0.0 copy-start.1
  2.0 1.0 %copy-done.1 = bf16[1024,256]{1,0:T(8,128)(2,1)S(1)} copy-done((bf16[1024,256]{1,0:T(8,128)(2,1)S(1)}, bf16[1024,256]{1,0:T(8,128)(2,1)}, u32[]{:S(2)}) %copy-start.1) | copy-done | bytes 524312
  3.1 0.0 copy-start.2
  3.1 0.7 copy-done.2
  3.8 0.0 copy-start.3
  3.8 0.7 copy-done.3
  4.5 76.5 %shard_map.59 = (bf16[1024,256]{1,0:T(8,128)(2,1)S(1)}, bf16[1024,256]{1,0:T(8,128)(2,1)S(1)}) custom-call(bf16[3,1024,256]{2,1,0:T(8,128)(2,1)S(1)} %copy-done, f32[3,1024]{1,0:T(4,128)S(1)} %copy-done.2, bf16[1024,256]{1,0:T(8,128)(2,1)S(1)} %copy-done.1, s32[2,2,32]{2,1,0:T(2,128)S(1)} %copy-done.3), custom_call_target="tpu_custom_call" | custom-call | tf_op jit(solution)/shard_map/pallas_call | solution.py:427
  81.0 0.8 copy.8
  81.8 0.8 copy.9
Async XLA Ops:
  0.6 1.4 %copy-start = (bf16[3,1024,256]{2,1,0:T(8,128)(2,1)S(1)}, bf16[3,1024,256]{2,1,0:T(8,128)(2,1)}, u32[]{:S(2)}) copy-start(bf16[3,1024,256]{2,1,0:T(8,128)(2,1)} %emb.1) | copy-start | bytes 4718596
  2.0 1.0 %copy-start.1 = (bf16[1024,256]{1,0:T(8,128)(2,1)S(1)}, bf16[1024,256]{1,0:T(8,128)(2,1)}, u32[]{:S(2)}) copy-start(bf16[1024,256]{1,0:T(8,128)(2,1)} %sig.1) | copy-start | bytes 1572868
  3.1 0.7 copy-start.2
  3.8 0.7 copy-start.3
where the time goes:
time: 82.9 us; the launch traced here: 82.6 us
  Pallas kernels  76.5 us (92%)
  local copies, waits for them, and re-layouts  5.43 us (7%)
    pallas_call x1, Pallas kernels, on_device(): pl.pallas_call(functools.partial(kernel, tiles), out_shape=(jax.ShapeDtyp...  76.5 us
    unnamed x10, local copies, waits for them, and re-layouts  5.43 us

commit v1 on v0

--- a/solution.py
+++ b/solution.py
@@ -53,9 +53,11 @@
     col_send,
     col_near,
     col_far,
-    part_send,
-    part_recv,
-    own_part,
+    a_send,
+    a_recv,
+    b_send,
+    b_recv,
+    kept,
     early_own,
     send_sem,
     recv_sem,
@@ -84,13 +86,16 @@
         return jnp.logical_and(c + offset >= 0, c + offset < n)
 
     def to_tile(src, dst, step):
+        return to_peer(src, dst, lax.rem(t + step, tiles))
+
+    def to_peer(src, dst, peer):
         i = fresh()
         copy = pltpu.make_async_remote_copy(
             src_ref=src,
             dst_ref=dst,
             send_sem=send_sem.at[i],
             recv_sem=recv_sem.at[i],
-            device_id={"tiles": lax.rem(t + step, tiles)},
+            device_id={"tiles": peer},
             device_id_type=pl.DeviceIdType.MESH,
         )
         copy.start()
@@ -128,7 +133,8 @@
             for k in range(2):
                 ys[k, part] = jnp.zeros(ys.shape[2:], BF16)
             fates_1[part] = jnp.zeros(fates_1.shape[1:], BF16)
-            fates_0[part] = jnp.zeros(fates_0.shape[1:], BF16)
+            for f in range(2):
+                fates_0[f, part] = jnp.zeros(fates_0.shape[2:], BF16)
             lm_win[part] = jnp.zeros(lm_win.shape[1:], F32)
 
     for buffer in (col_near, col_far):
@@ -179,8 +185,6 @@
     lm_waits = [to_cell(lm_src, lm_win.at[part], offset) for offset, part in near]
     y_waits = [None, None]
     y_waits[1] = [to_cell(emb.at[2, t_rows], ys.at[1, part], offset) for offset, part in near]
-    y_waits[0] = [to_cell(emb.at[1, t_rows], ys.at[0, part], offset) for offset, part in near]
-    sig_waits = [to_cell(sig.at[t_rows], fates_1.at[part], offset) for offset, part in near]
 
     lists[0] = listing[...]
     for wait in list_waits:
@@ -323,8 +327,13 @@
         wait()
     row_waits, col_waits = {}, {}
     for k in (1, 0):
-        for wait, (_, part) in zip(y_waits[k], near):
+        for wait in y_waits[k]:
             wait()
+        if k == 1:
+            y_waits[0] = [to_cell(emb.at[1, t_rows], ys.at[0, part], offset) for offset, part in near]
+        else:
+            sig_waits = [to_cell(sig.at[t_rows], fates_1.at[part], offset) for offset, part in near]
+        for _, part in near:
             products(k, part)
         for part in range(3):
             h_row[k, part] = lm_win[part, k] - y_norm[k, part]
@@ -354,17 +363,55 @@
     local[4].wait()
     for wait in sig_waits:
         wait()
-    part_waits = []
-    for step in range(1, tiles + 1):
-        block = row_block(lax.rem(t + step, tiles))
-        total = sum(
+    t_1 = t + 1 - 2 * lax.rem(t, 2)
+    t_2 = lax.rem(t + 2, tiles)
+    t_3 = lax.rem(t_1 + 2, tiles)
+    half = fates_0.shape[3]
+    lanes = [slice(f * half, (f + 1) * half) for f in range(2)]
+
+    def late_part(index):
+        block = row_block(index)
+        return sum(
             jnp.dot(weights(1, block, part), fates_1[part], preferred_element_type=F32) for part in range(3)
         )
-        if step < tiles:
-            part_send[1, step - 1] = total.astype(BF16)
-            part_waits.append(to_tile(part_send.at[1, step - 1], part_recv.at[1, step - 1], step))
-        else:
-            own_part[...] = total
+
+    def early_part(index, f):
+        block = row_block(index)
+        return sum(
+            jnp.dot(w_0[part, block, :], fates_0[f, part], preferred_element_type=F32) for part in range(3)
+        )
+
+    def to_mate(k, f):
+        return to_peer(a_send.at[k, f], a_recv.at[k, f], t_1)
+
+    def across(k, f, arrived):
+        arrived()
+        b_send[k, f] = (kept[k, f, 1] + a_recv[k, f, 1].astype(F32)).astype(BF16)
+        return to_peer(b_send.at[k, f], b_recv.at[k, f], t_2)
+
+    def summed(k, f, arrived):
+        arrived()
+        return (kept[k, f, 0] + a_recv[k, f, 0].astype(F32) + b_recv[k, f].astype(F32)).astype(BF16)
+
+    def gather(block, out, f):
+        here = out.at[t_rows, lanes[f]]
+        return to_peer(block, here, t_1), to_peer(block, here, t_2)
+
+    def forward(waits, out, f):
+        waits[1]()
+        there = out.at[row_block(t_2), lanes[f]]
+        return [waits[0], to_peer(there, there, t_1)]
+
+    for i, index in enumerate((t_1, t_3)):
+        total = late_part(index)
+        for f in range(2):
+            a_send[1, f, i] = total[:, lanes[f]].astype(BF16)
+    a_waits = [to_mate(1, f) for f in range(2)]
+    for i, index in enumerate((t, t_2)):
+        total = late_part(index)
+        for f in range(2):
+            kept[1, f, i] = total[:, lanes[f]]
+    b_waits = [across(1, f, a_waits[f]) for f in range(2)]
 
     spread(0, row_total(0, SWEEPS, row_waits[0]))
 
@@ -374,35 +421,33 @@
         for part in range(3):
             w_0[part, block, :] = weights(0, block, part)
 
-    for wait in part_waits:
-        wait()
-    fates_0[1] = (
-        own_part[...] + sum(part_recv[1, s].astype(F32) for s in range(tiles - 1))
-    ).astype(BF16)
-    late_waits = [to_cell(fates_0.at[1], fates_0.at[part], offset) for offset, part in near]
-    gather_waits = [to_tile(fates_0.at[1], late.at[t_rows], step) for step in range(1, tiles)]
-    late[t_rows, :] = fates_0[1]
-
-    for wait in late_waits:
-        wait()
-    part_waits = []
-    for step in range(1, tiles + 1):
-        block = row_block(lax.rem(t + step, tiles))
-        total = sum(
-            jnp.dot(w_0[part, block, :], fates_0[part], preferred_element_type=F32) for part in range(3)
-        )
-        if step < tiles:
-            part_send[0, step - 1] = total.astype(BF16)
-            part_waits.append(to_tile(part_send.at[0, step - 1], part_recv.at[0, step - 1], step))
-        else:
-            own_part[...] = total
-    for wait in part_waits:
-        wait()
-    early_own[...] = (
-        own_part[...] + sum(part_recv[0, s].astype(F32) for s in range(tiles - 1))
-    ).astype(BF16)
-    gather_waits += [to_tile(early_own, early.at[t_rows], step) for step in range(1, tiles)]
-    early[t_rows, :] = early_own[...]
+    late_waits, late_gather = [], []
+    for f in range(2):
+        fates_0[f, 1] = summed(1, f, b_waits[f])
+        late_waits.append([to_cell(fates_0.at[f, 1], fates_0.at[f, part], offset) for offset, part in near])
+        late_gather.append(gather(fates_0.at[f, 1], late, f))
+        late[t_rows, lanes[f]] = fates_0[f, 1]
+
+    b_waits = []
+    for f in range(2):
+        for wait in late_waits[f]:
+            wait()
+        for i, index in enumerate((t_1, t_3)):
+            a_send[0, f, i] = early_part(index, f).astype(BF16)
+        arrived = to_mate(0, f)
+        for i, index in enumerate((t, t_2)):
+            kept[0, f, i] = early_part(index, f)
+        b_waits.append(across(0, f, arrived))
+    gather_waits = []
+    for f in range(2):
+        gather_waits += forward(late_gather[f], late, f)
+    early_gather = []
+    for f in range(2):
+        early_own[f] = summed(0, f, b_waits[f])
+        early_gather.append(gather(early_own.at[f], early, f))
+        early[t_rows, lanes[f]] = early_own[f]
+    for f in range(2):
+        gather_waits += forward(early_gather[f], early, f)
     for wait in gather_waits:
         wait()
     for copy, offset in sends:
@@ -443,7 +488,7 @@
             vmem((2, n_tgt, rows, BLOCK), F32),
             vmem((2, n_src, n_tgt * BLOCK, BLOCK), F32),
             vmem((3, q_rows, fate), BF16),
-            vmem((3, q_rows, fate), BF16),
+            vmem((2, 3, q_rows, fate // 2), BF16),
             vmem((3, rows, q_rows), BF16),
             vmem((tiles,) + tile_list.shape, jnp.int32),
             vmem((2, 8, BLOCK), F32),
@@ -459,10 +504,12 @@
             vmem((2, SWEEPS, 3, 2, 8, BLOCK), F32),
             vmem((2, SWEEPS, 2, 2, 2, 8, BLOCK), F32),
             vmem((2, SWEEPS, 2, 1, 2, 8, BLOCK), F32),
-            vmem((2, tiles - 1, q_rows, fate), BF16),
-            vmem((2, tiles - 1, q_rows, fate), BF16),
-            vmem((q_rows, fate), F32),
-            vmem((q_rows, fate), BF16),
+            vmem((2, 2, 2, q_rows, fate // 2), BF16),
+            vmem((2, 2, 2, q_rows, fate // 2), BF16),
+            vmem((2, 2, q_rows, fate // 2), BF16),
+            vmem((2, 2, q_rows, fate // 2), BF16),
+            vmem((2, 2, 2, q_rows, fate // 2), F32),
+            vmem((2, q_rows, fate // 2), BF16),
             pltpu.SemaphoreType.DMA((copies,)),
             pltpu.SemaphoreType.DMA((copies,)),
             pltpu.SemaphoreType.DMA((5,)),

time: 82.9 us -> 74 us (0.89)
  Pallas kernels: 76.5 us -> 67.6 us
    pallas_call x1, Pallas kernels: 76.5 us -> 67.6 us  [on_device(): pl.pallas_call(functools.partial(kernel, tiles), out_shape=(jax.ShapeDtyp...]
where the time goes in v1:
time: 74 us; the launch traced here: 73.7 us
  Pallas kernels  67.6 us (91%)
  local copies, waits for them, and re-layouts  5.43 us (7%)
    pallas_call x1, Pallas kernels, on_device(): pl.pallas_call(functools.partial(kernel, tiles), out_shape=(jax.ShapeDtyp...  67.6 us
    unnamed x10, local copies, waits for them, and re-layouts  5.43 us

profile of v1, /device:TPU:9, one launch (start us, length us, event | category | flops | bytes accessed | tf_op | source)
XLA Modules:
  0.0 73.7 jit_solution(10598127574401770406)
XLA Ops:
  0.6 0.0 copy-start
  0.6 1.4 %copy-done = bf16[3,1024,256]{2,1,0:T(8,128)(2,1)S(1)} copy-done((bf16[3,1024,256]{2,1,0:T(8,128)(2,1)S(1)}, bf16[3,1024,256]{2,1,0:T(8,128)(2,1)}, u32[]{:S(2)}) %copy-start) | copy-done | bytes 1572888
  2.0 0.0 copy-start.1
  2.0 1.0 %copy-done.1 = bf16[1024,256]{1,0:T(8,128)(2,1)S(1)} copy-done((bf16[1024,256]{1,0:T(8,128)(2,1)S(1)}, bf16[1024,256]{1,0:T(8,128)(2,1)}, u32[]{:S(2)}) %copy-start.1) | copy-done | bytes 524312
  3.1 0.0 copy-start.2
  3.1 0.7 copy-done.2
  3.8 0.0 copy-start.3
  3.8 0.7 copy-done.3
  4.5 67.6 %shard_map.59 = (bf16[1024,256]{1,0:T(8,128)(2,1)S(1)}, bf16[1024,256]{1,0:T(8,128)(2,1)S(1)}) custom-call(bf16[3,1024,256]{2,1,0:T(8,128)(2,1)S(1)} %copy-done, f32[3,1024]{1,0:T(4,128)S(1)} %copy-done.2, bf16[1024,256]{1,0:T(8,128)(2,1)S(1)} %copy-done.1, s32[2,2,32]{2,1,0:T(2,128)S(1)} %copy-done.3), custom_call_target="tpu_custom_call" | custom-call | tf_op jit(solution)/shard_map/pallas_call | solution.py:472
  72.1 0.8 %copy.8 = bf16[1024,256]{1,0:T(8,128)(2,1)} copy(bf16[1024,256]{1,0:T(8,128)(2,1)S(1)} %get-tuple-element.4) | data formatting | bytes 1048576
  72.9 0.8 %copy.9 = bf16[1024,256]{1,0:T(8,128)(2,1)} copy(bf16[1024,256]{1,0:T(8,128)(2,1)S(1)} %get-tuple-element.5) | data formatting | bytes 1048576
Async XLA Ops:
  0.6 1.4 %copy-start = (bf16[3,1024,256]{2,1,0:T(8,128)(2,1)S(1)}, bf16[3,1024,256]{2,1,0:T(8,128)(2,1)}, u32[]{:S(2)}) copy-start(bf16[3,1024,256]{2,1,0:T(8,128)(2,1)} %emb.1) | copy-start | bytes 4718596
  2.0 1.0 %copy-start.1 = (bf16[1024,256]{1,0:T(8,128)(2,1)S(1)}, bf16[1024,256]{1,0:T(8,128)(2,1)}, u32[]{:S(2)}) copy-start(bf16[1024,256]{1,0:T(8,128)(2,1)} %sig.1) | copy-start | bytes 1572868
  3.1 0.7 copy-start.2
  3.8 0.7 copy-start.3

commit v2 on v1

--- a/solution.py
+++ b/solution.py
@@ -27,7 +27,7 @@
 def kernel(
     tiles,
     emb,
-    log_mass,
+    log_mass_in,
     sig,
     listing,
     early,
@@ -40,6 +40,7 @@
     fates_0,
     w_0,
     lists,
+    log_mass,
     lm_src,
     lm_win,
     bias,
@@ -164,12 +165,15 @@
             (emb.at[0], xs.at[0]),
             (emb.at[1, t_rows], ys.at[0, 1]),
             (sig.at[t_rows], fates_1.at[1]),
+            (log_mass_in, log_mass),
+            (listing, lists.at[0]),
         )
     ):
         copy = pltpu.make_async_copy(src, dst, local_sem.at[i])
         copy.start()
         local.append(copy)
 
+    local[5].wait()
     lm_src[...] = jnp.zeros(lm_src.shape, F32)
     for k in range(2):
         for q in range(n_q):
@@ -186,7 +190,7 @@
     y_waits = [None, None]
     y_waits[1] = [to_cell(emb.at[2, t_rows], ys.at[1, part], offset) for offset, part in near]
 
-    lists[0] = listing[...]
+    local[6].wait()
     for wait in list_waits:
         wait()
 
@@ -203,40 +207,57 @@
             found = found + jnp.sum(jnp.where(hit, 1.0, 0.0), axis=1, keepdims=True)
         bias[k] = jnp.broadcast_to(jnp.where(found > 0.0, 0.0, NEG), (n_src * n_tgt, BLOCK))
 
-    ones = jnp.ones((8, depth), BF16)
-
-    def norm_rows(block):
+    def norm_row(block):
         wide = block.astype(F32)
         square = wide * wide
-        high = square.astype(BF16)
-        low = (square - high.astype(F32)).astype(BF16)
-        return scale * (
-            lax.dot_general(ones, high, NT, preferred_element_type=F32)
-            + lax.dot_general(ones, low, NT, preferred_element_type=F32)
-        )
+        folded = sum(square[:, e : e + BLOCK] for e in range(0, depth, BLOCK))
+        return scale * jnp.sum(jnp.transpose(folded), axis=0, keepdims=True)
 
     def source_norms(k):
         @pl.loop(0, n_src)
         def _(b):
-            x_norm[k, pl.ds(b, 1), :] = norm_rows(xs[k, pl.ds(pl.multiple_of(b * BLOCK, BLOCK), BLOCK), :])[0:1]
+            x_norm[k, pl.ds(b, 1), :] = norm_row(xs[k, pl.ds(pl.multiple_of(b * BLOCK, BLOCK), BLOCK), :])
 
     def products(k, part):
         y = ys[k, part]
-        norms = norm_rows(y)
         for q in range(n_q):
-            y_norm[k, part, q : q + 1, :] = norms[0:1, q * BLOCK : (q + 1) * BLOCK]
-
-        @pl.loop(0, n_src)
-        def _(b):
-            block = pl.ds(pl.multiple_of(b * BLOCK, BLOCK), BLOCK)
-            x = xs[k, block, :]
+            y_norm[k, part, q : q + 1, :] = norm_row(y[q * BLOCK : (q + 1) * BLOCK])
+
+        @pl.loop(0, n_src // 2)
+        def _(pair_index):
+            x = xs[k, pl.ds(pl.multiple_of(pair_index * 2 * BLOCK, 2 * BLOCK), 2 * BLOCK), :]
             cross = lax.dot_general(x, y, NT, preferred_element_type=F32) * (2.0 * scale)
             crossed = lax.dot_general(y, x, NT, preferred_element_type=F32) * (2.0 * scale)
-            for q in range(n_q):
-                j = part * n_q + q
-                shift = bias[k, pl.ds(b * n_tgt + j, 1), :]
-                d[k, j, block, :] = cross[:, q * BLOCK : (q + 1) * BLOCK] + shift
-                dt[k, b, j * BLOCK : (j + 1) * BLOCK, :] = crossed[q * BLOCK : (q + 1) * BLOCK] + shift
+            for side in range(2):
+                b = pair_index * 2 + side
+                block = pl.ds(pl.multiple_of(b * BLOCK, BLOCK), BLOCK)
+                own = slice(side * BLOCK, (side + 1) * BLOCK)
+                for q in range(n_q):
+                    j = part * n_q + q
+                    shift = bias[k, pl.ds(b * n_tgt + j, 1), :]
+                    other = slice(q * BLOCK, (q + 1) * BLOCK)
+                    d[k, j, block, :] = cross[own, other] + shift
+                    dt[k, b, j * BLOCK : (j + 1) * BLOCK, :] = crossed[other, own] + shift
+
+    def fold(combine, slabs):
+        value = functools.reduce(combine, slabs)
+        while value.shape[0] > 1:
+            middle = value.shape[0] // 2
+            value = combine(value[:middle], value[middle:])
+        return value
+
+    def log_sum(terms, products_of, count):
+        slabs = [
+            (terms[b * BLOCK : (b + 1) * BLOCK, :] + products_of[b * BLOCK : (b + 1) * BLOCK, :]).reshape(
+                BLOCK // 8, 8, BLOCK
+            )
+            for b in range(count)
+        ]
+        high = fold(jnp.maximum, slabs)
+        mass = fold(jnp.add, [jnp.exp2(slab - high) for slab in slabs])[0]
+        high = high[0]
+        highest = jnp.max(high, axis=0, keepdims=True)
+        return highest, jnp.sum(mass * jnp.exp2(high - highest), axis=0, keepdims=True)
 
     def down(row):
         return jnp.transpose(jnp.broadcast_to(row, (BLOCK, BLOCK)))
@@ -245,12 +266,13 @@
         for j in range(n_tgt):
             hb[k, j * BLOCK : (j + 1) * BLOCK, :] = down(h_row[k, j // n_q, j % n_q : j % n_q + 1, :])
 
-        @pl.loop(0, n_src)
-        def _(b):
-            scores = hb[k] + dt[k, b]
-            highest = jnp.max(scores, axis=0, keepdims=True)
-            row_send[k, phase, 0, pl.ds(b, 1), :] = highest
-            row_send[k, phase, 1, pl.ds(b, 1), :] = jnp.sum(jnp.exp2(scores - highest), axis=0, keepdims=True)
+        @pl.loop(0, n_src // 2)
+        def _(pair_index):
+            for side in range(2):
+                b = pair_index * 2 + side
+                highest, mass = log_sum(hb.at[k], dt.at[k, b], n_tgt)
+                row_send[k, phase, 0, pl.ds(b, 1), :] = highest
+                row_send[k, phase, 1, pl.ds(b, 1), :] = mass
 
         return [
             to_tile(row_send.at[k, phase], row_recv.at[k, phase, step - 1], step) for step in range(1, tiles)
@@ -281,12 +303,9 @@
         @pl.loop(0, 3)
         def _(part):
             for q in range(n_q):
-                scores = ub[k] + d[k, part * n_q + q]
-                highest = jnp.max(scores, axis=0, keepdims=True)
+                highest, mass = log_sum(ub.at[k], d.at[k, part * n_q + q], n_src)
                 col_send[k, phase, part, 0, q : q + 1, :] = highest
-                col_send[k, phase, part, 1, q : q + 1, :] = jnp.sum(
-                    jnp.exp2(scores - highest), axis=0, keepdims=True
-                )
+                col_send[k, phase, part, 1, q : q + 1, :] = mass
 
         mine = col_send.at[k, phase]
         return [
@@ -475,12 +494,7 @@
             jax.ShapeDtypeStruct((rows, fate), BF16),
             jax.ShapeDtypeStruct((rows, fate), BF16),
         ),
-        in_specs=[
-            pl.BlockSpec(memory_space=pl.ANY),
-            pl.BlockSpec(memory_space=vmem),
-            pl.BlockSpec(memory_space=pl.ANY),
-            pl.BlockSpec(memory_space=vmem),
-        ],
+        in_specs=[pl.BlockSpec(memory_space=pltpu.HBM)] * 4,
         out_specs=(pl.BlockSpec(memory_space=vmem), pl.BlockSpec(memory_space=vmem)),
         scratch_shapes=[
             vmem((2, rows, depth), BF16),
@@ -491,6 +505,7 @@
             vmem((2, 3, q_rows, fate // 2), BF16),
             vmem((3, rows, q_rows), BF16),
             vmem((tiles,) + tile_list.shape, jnp.int32),
+            vmem(log_mass.shape, F32),
             vmem((2, 8, BLOCK), F32),
             vmem((3, 2, 8, BLOCK), F32),
             vmem((2, n_src * n_tgt, BLOCK), F32),
@@ -512,10 +527,10 @@
             vmem((2, q_rows, fate // 2), BF16),
             pltpu.SemaphoreType.DMA((copies,)),
             pltpu.SemaphoreType.DMA((copies,)),
-            pltpu.SemaphoreType.DMA((5,)),
+            pltpu.SemaphoreType.DMA((7,)),
         ],
         compiler_params=pltpu.CompilerParams(
-            collective_id=0, has_side_effects=True, vmem_limit_bytes=44 * 1024 * 1024
+            collective_id=0, has_side_effects=True, vmem_limit_bytes=58 * 1024 * 1024
         ),
     )(embeddings, log_mass, signatures, tile_list)
 

time: 74 us -> 67.1 us (0.907)
  Pallas kernels: 67.6 us -> 62.3 us
  local copies, waits for them, and re-layouts: 5.43 us -> 3.74 us
    pallas_call x1, Pallas kernels: 67.6 us -> 62.3 us  [on_device(): pl.pallas_call(functools.partial(kernel, tiles), out_shape=(jax.ShapeDtyp...]
    unnamed x10 -> x2, local copies, waits for them, and re-layouts: 5.43 us -> 3.74 us
where the time goes in v2:
time: 67.1 us; the launch traced here: 66.6 us
  Pallas kernels  62.3 us (93%)
  local copies, waits for them, and re-layouts  3.74 us (6%)
    pallas_call x1, Pallas kernels, on_device(): pl.pallas_call(functools.partial(kernel, tiles), out_shape=(jax.ShapeDtyp...  62.3 us
    unnamed x2, local copies, waits for them, and re-layouts  3.74 us

profile of v2, /device:TPU:9, one launch (start us, length us, event | category | flops | bytes accessed | tf_op | source)
XLA Modules:
  0.0 66.6 jit_solution(12345902381855042213)
XLA Ops:
  0.6 62.3 %shard_map.59 = (bf16[1024,256]{1,0:T(8,128)(2,1)}, bf16[1024,256]{1,0:T(8,128)(2,1)}) custom-call(bf16[3,1024,256]{2,1,0:T(8,128)(2,1)} %emb.1, f32[3,1024]{1,0:T(4,128)} %log_mass_in.1, bf16[1024,256]{1,0:T(8,128)(2,1)} %sig.1, s32[2,2,32]{2,1,0:T(2,128)} %listing.1), custom_call_target="tpu_custom_call" | custom-call | tf_op jit(solution)/shard_map/pallas_call | solution.py:491
  62.9 1.9 %copy.8 = bf16[1024,256]{1,0:T(8,128)(2,1)} copy(bf16[1024,256]{1,0:T(8,128)(2,1)} %get-tuple-element.4) | data formatting | bytes 1048576
  64.8 1.9 %copy.9 = bf16[1024,256]{1,0:T(8,128)(2,1)} copy(bf16[1024,256]{1,0:T(8,128)(2,1)} %get-tuple-element.5) | data formatting | bytes 1048576

commit v3 on v2

--- a/solution.py
+++ b/solution.py
@@ -21,7 +21,7 @@
 
 
 def copy_count(tiles):
-    return tiles * 12 + 40
+    return tiles * 12 + 48
 
 
 def kernel(
@@ -103,7 +103,8 @@
         sends.append((copy, None))
         return copy.wait_recv
 
-    def to_cell(src, dst, offset):
+    def to_cell(src, dst, offset, origin=None):
+        origin = -offset if origin is None else origin
         i = fresh()
         copy = pltpu.make_async_remote_copy(
             src_ref=src,
@@ -121,7 +122,7 @@
         sends.append((copy, offset))
 
         def wait():
-            @pl.when(present(-offset))
+            @pl.when(present(origin))
             def _():
                 copy.wait_recv()
 
@@ -187,8 +188,29 @@
     list_waits = [to_tile(listing, lists.at[step], step) for step in range(1, tiles)]
     near = ((1, 0), (-1, 2))
     lm_waits = [to_cell(lm_src, lm_win.at[part], offset) for offset, part in near]
-    y_waits = [None, None]
-    y_waits[1] = [to_cell(emb.at[2, t_rows], ys.at[1, part], offset) for offset, part in near]
+
+    odd = lax.rem(c, 2)
+    mate = 1 - 2 * odd
+    part_in, part_out = 2 - 2 * odd, 2 * odd
+
+    def to_pair(pieces):
+        return [(to_cell(src, buffer.at[part_out], mate, mate), buffer) for src, buffer in pieces]
+
+    def hand_on(arrivals):
+        waits = []
+        for arrived, buffer in arrivals:
+            arrived()
+            waits.append(to_cell(buffer.at[part_in], buffer.at[part_out], 2 * mate))
+        return waits
+
+    def embedding_pieces(k):
+        pieces = []
+        for q in range(n_q):
+            start = pl.multiple_of(t * q_rows + q * BLOCK, BLOCK)
+            pieces.append((emb.at[k + 1, pl.ds(start, BLOCK)], ys.at[k, :, pl.ds(q * BLOCK, BLOCK)]))
+        return pieces
+
+    y_arrivals = to_pair(embedding_pieces(1))
 
     local[6].wait()
     for wait in list_waits:
@@ -237,7 +259,7 @@
                     shift = bias[k, pl.ds(b * n_tgt + j, 1), :]
                     other = slice(q * BLOCK, (q + 1) * BLOCK)
                     d[k, j, block, :] = cross[own, other] + shift
-                    dt[k, b, j * BLOCK : (j + 1) * BLOCK, :] = crossed[other, own] + shift
+                    dt[k, b, pl.ds(pl.multiple_of(j * BLOCK, BLOCK), BLOCK), :] = crossed[other, own] + shift
 
     def fold(combine, slabs):
         value = functools.reduce(combine, slabs)
@@ -345,24 +367,37 @@
     for wait in lm_waits:
         wait()
     row_waits, col_waits = {}, {}
-    for k in (1, 0):
-        for wait in y_waits[k]:
+
+    def first_rows(k, y_waits):
+        products(k, part_in)
+        for wait in y_waits:
             wait()
-        if k == 1:
-            y_waits[0] = [to_cell(emb.at[1, t_rows], ys.at[0, part], offset) for offset, part in near]
-        else:
-            sig_waits = [to_cell(sig.at[t_rows], fates_1.at[part], offset) for offset, part in near]
-        for _, part in near:
-            products(k, part)
+        products(k, part_out)
         for part in range(3):
             h_row[k, part] = lm_win[part, k] - y_norm[k, part]
         row_waits[k] = row_pass(k, 0)
+
+    def columns(k, sweep):
+        col_waits[k] = col_pass(k, sweep, row_total(k, sweep, row_waits[k]))
+
+    def next_rows(k, sweep):
+        col_total(k, sweep, col_waits[k])
+        row_waits[k] = row_pass(k, sweep + 1)
+
+    y_waits = hand_on(y_arrivals)
+    y_arrivals = to_pair(embedding_pieces(0))
+    first_rows(1, y_waits)
+    y_waits = hand_on(y_arrivals)
+    sig_arrivals = to_pair([(sig.at[t_rows], fates_1)])
+    columns(1, 0)
+    first_rows(0, y_waits)
+    sig_waits = hand_on(sig_arrivals)
     for sweep in range(SWEEPS):
-        for k in (1, 0):
-            col_waits[k] = col_pass(k, sweep, row_total(k, sweep, row_waits[k]))
-        for k in (1, 0):
-            col_total(k, sweep, col_waits[k])
-            row_waits[k] = row_pass(k, sweep + 1)
+        next_rows(1, sweep)
+        columns(0, sweep)
+        if sweep + 1 < SWEEPS:
+            columns(1, sweep + 1)
+            next_rows(0, sweep)
 
     def weights(k, block, part):
         return jnp.concatenate(
@@ -432,20 +467,23 @@
             kept[1, f, i] = total[:, lanes[f]]
     b_waits = [across(1, f, a_waits[f]) for f in range(2)]
 
+    next_rows(0, SWEEPS - 1)
+
+    late_arrivals, late_gather = [], []
+    for f in range(2):
+        fates_0[f, 1] = summed(1, f, b_waits[f])
+        late_arrivals.append(to_pair([(fates_0.at[f, 1], fates_0.at[f])]))
+        late_gather.append(gather(fates_0.at[f, 1], late, f))
+        late[t_rows, lanes[f]] = fates_0[f, 1]
+
     spread(0, row_total(0, SWEEPS, row_waits[0]))
+    late_waits = [hand_on(late_arrivals[f]) for f in range(2)]
 
     @pl.loop(0, tiles)
     def _(r):
         block = row_block(r)
         for part in range(3):
             w_0[part, block, :] = weights(0, block, part)
-
-    late_waits, late_gather = [], []
-    for f in range(2):
-        fates_0[f, 1] = summed(1, f, b_waits[f])
-        late_waits.append([to_cell(fates_0.at[f, 1], fates_0.at[f, part], offset) for offset, part in near])
-        late_gather.append(gather(fates_0.at[f, 1], late, f))
-        late[t_rows, lanes[f]] = fates_0[f, 1]
 
     b_waits = []
     for f in range(2):

time: 67.1 us -> 67.1 us (level)
  no operation moved by 1% of the time
where the time goes in v3:
time: 67.1 us; the launch traced here: 66.7 us
  Pallas kernels  62.4 us (93%)
  local copies, waits for them, and re-layouts  3.74 us (6%)
    pallas_call x1, Pallas kernels, on_device(): pl.pallas_call(functools.partial(kernel, tiles), out_shape=(jax.ShapeDtyp...  62.4 us
    unnamed x2, local copies, waits for them, and re-layouts  3.74 us

profile of v3, /device:TPU:9, one launch (start us, length us, event | category | flops | bytes accessed | tf_op | source)
XLA Modules:
  0.0 66.7 jit_solution(14000974062622431808)
XLA Ops:
  0.6 62.4 %shard_map.59 = (bf16[1024,256]{1,0:T(8,128)(2,1)}, bf16[1024,256]{1,0:T(8,128)(2,1)}) custom-call(bf16[3,1024,256]{2,1,0:T(8,128)(2,1)} %emb.1, f32[3,1024]{1,0:T(4,128)} %log_mass_in.1, bf16[1024,256]{1,0:T(8,128)(2,1)} %sig.1, s32[2,2,32]{2,1,0:T(2,128)} %listing.1), custom_call_target="tpu_custom_call" | custom-call | tf_op jit(solution)/shard_map/pallas_call | solution.py:529
  63.0 1.9 %copy.8 = bf16[1024,256]{1,0:T(8,128)(2,1)} copy(bf16[1024,256]{1,0:T(8,128)(2,1)} %get-tuple-element.4) | data formatting | bytes 1048576
  64.9 1.9 %copy.9 = bf16[1024,256]{1,0:T(8,128)(2,1)} copy(bf16[1024,256]{1,0:T(8,128)(2,1)} %get-tuple-element.5) | data formatting | bytes 1048576

commit v4 on v3

--- a/solution.py
+++ b/solution.py
@@ -281,12 +281,15 @@
         highest = jnp.max(high, axis=0, keepdims=True)
         return highest, jnp.sum(mass * jnp.exp2(high - highest), axis=0, keepdims=True)
 
-    def down(row):
-        return jnp.transpose(jnp.broadcast_to(row, (BLOCK, BLOCK)))
+    def down(target, values):
+        count = values.shape[0]
+        tall = jnp.transpose(jnp.concatenate([values] * (BLOCK // count), axis=0))
+        for b in range(count):
+            target[b * BLOCK : (b + 1) * BLOCK, :] = jnp.broadcast_to(tall[:, b : b + 1], (BLOCK, BLOCK))
 
     def row_pass(k, phase):
-        for j in range(n_tgt):
-            hb[k, j * BLOCK : (j + 1) * BLOCK, :] = down(h_row[k, j // n_q, j % n_q : j % n_q + 1, :])
+        filler = [jnp.zeros((8 - n_tgt, BLOCK), F32)]
+        down(hb.at[k], jnp.concatenate([h_row[k, part, 0:n_q, :] for part in range(3)] + filler, axis=0))
 
         @pl.loop(0, n_src // 2)
         def _(pair_index):
@@ -313,8 +316,7 @@
         return merged(pairs)
 
     def spread(k, values):
-        for b in range(n_src):
-            ub[k, b * BLOCK : (b + 1) * BLOCK, :] = down(values[b : b + 1])
+        down(ub.at[k], values)
 
     def col_pass(k, phase, total):
         mass = jnp.concatenate(
@@ -550,7 +552,7 @@
             vmem((2, n_src, BLOCK), F32),
             vmem((2, 3, 8, BLOCK), F32),
             vmem((2, 3, 8, BLOCK), F32),
-            vmem((2, n_tgt * BLOCK, BLOCK), F32),
+            vmem((2, 8 * BLOCK, BLOCK), F32),
             vmem((2, rows, BLOCK), F32),
             vmem((2, SWEEPS + 1, 2, n_src, BLOCK), F32),
             vmem((2, SWEEPS + 1, tiles - 1, 2, n_src, BLOCK), F32),

time: 67.1 us -> 68.1 us (1.015)
  Pallas kernels: 62.4 us -> 63.5 us
    pallas_call x1, Pallas kernels: 62.4 us -> 63.5 us  [on_device(): pl.pallas_call(functools.partial(kernel, tiles), out_shape=(jax.ShapeDtyp...]
where the time goes in v4:
time: 68.1 us; the launch traced here: 67.9 us
  Pallas kernels  63.5 us (93%)
  local copies, waits for them, and re-layouts  3.74 us (5%)
    pallas_call x1, Pallas kernels, on_device(): pl.pallas_call(functools.partial(kernel, tiles), out_shape=(jax.ShapeDtyp...  63.5 us
    unnamed x2, local copies, waits for them, and re-layouts  3.74 us

profile of v4, /device:TPU:9, one launch (start us, length us, event | category | flops | bytes accessed | tf_op | source)
XLA Modules:
  0.0 67.9 jit_solution(7146412433824227104)
XLA Ops:
  0.6 63.5 %shard_map.59 = (bf16[1024,256]{1,0:T(8,128)(2,1)}, bf16[1024,256]{1,0:T(8,128)(2,1)}) custom-call(bf16[3,1024,256]{2,1,0:T(8,128)(2,1)} %emb.1, f32[3,1024]{1,0:T(4,128)} %log_mass_in.1, bf16[1024,256]{1,0:T(8,128)(2,1)} %sig.1, s32[2,2,32]{2,1,0:T(2,128)} %listing.1), custom_call_target="tpu_custom_call" | custom-call | tf_op jit(solution)/shard_map/pallas_call | solution.py:531
  64.1 1.9 %copy.8 = bf16[1024,256]{1,0:T(8,128)(2,1)} copy(bf16[1024,256]{1,0:T(8,128)(2,1)} %get-tuple-element.4) | data formatting | bytes 1048576
  66.0 1.9 %copy.9 = bf16[1024,256]{1,0:T(8,128)(2,1)} copy(bf16[1024,256]{1,0:T(8,128)(2,1)} %get-tuple-element.5) | data formatting | bytes 1048576

commit v5 on v3

--- a/solution.py
+++ b/solution.py
@@ -210,7 +210,7 @@
             pieces.append((emb.at[k + 1, pl.ds(start, BLOCK)], ys.at[k, :, pl.ds(q * BLOCK, BLOCK)]))
         return pieces
 
-    y_arrivals = to_pair(embedding_pieces(1))
+    y_waits = [to_cell(emb.at[2, t_rows], ys.at[1, part], offset) for offset, part in near]
 
     local[6].wait()
     for wait in list_waits:
@@ -368,11 +368,9 @@
         wait()
     row_waits, col_waits = {}, {}
 
-    def first_rows(k, y_waits):
-        products(k, part_in)
-        for wait in y_waits:
-            wait()
-        products(k, part_out)
+    def first_rows(k):
+        for part in (part_in, part_out):
+            products(k, part)
         for part in range(3):
             h_row[k, part] = lm_win[part, k] - y_norm[k, part]
         row_waits[k] = row_pass(k, 0)
@@ -384,13 +382,16 @@
         col_total(k, sweep, col_waits[k])
         row_waits[k] = row_pass(k, sweep + 1)
 
-    y_waits = hand_on(y_arrivals)
+    for wait in y_waits:
+        wait()
     y_arrivals = to_pair(embedding_pieces(0))
-    first_rows(1, y_waits)
+    first_rows(1)
     y_waits = hand_on(y_arrivals)
     sig_arrivals = to_pair([(sig.at[t_rows], fates_1)])
     columns(1, 0)
-    first_rows(0, y_waits)
+    for wait in y_waits:
+        wait()
+    first_rows(0)
     sig_waits = hand_on(sig_arrivals)
     for sweep in range(SWEEPS):
         next_rows(1, sweep)
@@ -469,15 +470,14 @@
 
     next_rows(0, SWEEPS - 1)
 
-    late_arrivals, late_gather = [], []
+    late_waits, late_gather = [], []
     for f in range(2):
         fates_0[f, 1] = summed(1, f, b_waits[f])
-        late_arrivals.append(to_pair([(fates_0.at[f, 1], fates_0.at[f])]))
+        late_waits.append([to_cell(fates_0.at[f, 1], fates_0.at[f, part], offset) for offset, part in near])
         late_gather.append(gather(fates_0.at[f, 1], late, f))
         late[t_rows, lanes[f]] = fates_0[f, 1]
 
     spread(0, row_total(0, SWEEPS, row_waits[0]))
-    late_waits = [hand_on(late_arrivals[f]) for f in range(2)]
 
     @pl.loop(0, tiles)
     def _(r):

time: 67.1 us -> 63.8 us (0.951)
  Pallas kernels: 62.4 us -> 59.1 us
    pallas_call x1, Pallas kernels: 62.4 us -> 59.1 us  [on_device(): pl.pallas_call(functools.partial(kernel, tiles), out_shape=(jax.ShapeDtyp...]
where the time goes in v5:
time: 63.8 us; the launch traced here: 63.5 us
  Pallas kernels  59.1 us (93%)
  local copies, waits for them, and re-layouts  3.74 us (6%)
  between operations  0.64 us (1%)
    pallas_call x1, Pallas kernels, on_device(): pl.pallas_call(functools.partial(kernel, tiles), out_shape=(jax.ShapeDtyp...  59.1 us
    unnamed x2, local copies, waits for them, and re-layouts  3.74 us

profile of v5, /device:TPU:9, one launch (start us, length us, event | category | flops | bytes accessed | tf_op | source)
XLA Modules:
  0.0 63.5 jit_solution(16654756845133005652)
XLA Ops:
  0.6 59.1 %shard_map.59 = (bf16[1024,256]{1,0:T(8,128)(2,1)}, bf16[1024,256]{1,0:T(8,128)(2,1)}) custom-call(bf16[3,1024,256]{2,1,0:T(8,128)(2,1)} %emb.1, f32[3,1024]{1,0:T(4,128)} %log_mass_in.1, bf16[1024,256]{1,0:T(8,128)(2,1)} %sig.1, s32[2,2,32]{2,1,0:T(2,128)} %listing.1), custom_call_target="tpu_custom_call" | custom-call | tf_op jit(solution)/shard_map/pallas_call | solution.py:529
  59.8 1.9 %copy.8 = bf16[1024,256]{1,0:T(8,128)(2,1)} copy(bf16[1024,256]{1,0:T(8,128)(2,1)} %get-tuple-element.4) | data formatting | bytes 1048576
  61.6 1.9 %copy.9 = bf16[1024,256]{1,0:T(8,128)(2,1)} copy(bf16[1024,256]{1,0:T(8,128)(2,1)} %get-tuple-element.5) | data formatting | bytes 1048576
